TPU v7x, 256 devices: a whole 4x4x8 slice. The times are simulated.
256 devices in a mesh: seq: 64 (over y, x, z_lo), head: 4 (over z_hi, core).
Axes of the slice: x: 4, y: 4, z: 8 (z_hi: 2, z_lo: 4; z = z_hi * 4 + z_lo), core: 2. Of those that a mesh axis runs over, the one named last changes fastest.
Arguments:
- layer_input: bfloat16 [1, 128, 256, 1280], P(None, 'seq'), may hold values from -16 to 16
- cotangent: bfloat16 [1, 128, 256, 1280], P(None, 'seq'), may hold values from -16 to 16
- queries: bfloat16 [1, 128, 256, 1280], P(None, None, 'seq', 'head'), may hold values from -18 to 18
- keys: bfloat16 [1, 128, 256, 1280], P(None, None, 'seq', 'head'), may hold values from -6 to 6
- values: bfloat16 [1, 128, 256, 1280], P(None, None, 'seq', 'head'), may hold values from -6 to 6
- gain: float32 [1280], replicated, may hold values from 0.25 to 1.75
- w_qkv: bfloat16 [1280, 3, 1280], P('seq', None, 'head'), may hold values from -0.15625 to 0.15625
- w_out: bfloat16 [1280, 1280], P('head', 'seq'), may hold values from -0.15625 to 0.15625
Outputs:
- branch_input_gradient: bfloat16 [1, 128, 256, 1280], P(None, 'seq', None, 'head')
- grad_wqkv: float32 [1280, 3, 1280], P('seq', None, 'head')
- grad_wout: float32 [1280, 1280], P('head', 'seq')
- gain_gradient: float32 [1280], P('head')
All inputs are finite; a program needn't handle non-finite values.
Results may differ from a plain program's by a relative error of at most 0.0064.
Values may be sent and summed in bfloat16 or wider, within the bound.
No kernel may reach another device: no remote copies, remote signals or barrier semaphores. Data moves between devices by JAX's collectives and lax.ppermute only.
A program may use at most 64 MiB of HBM per device.

v0:
```python
import jax
import jax.numpy as jnp
from jax import lax
from jax.sharding import PartitionSpec as P

DH = 80


def attend_grad(queries, keys, values, grad_attn):
    video_batch, frames, patches, width = queries.shape
    heads = width // DH
    shape = (video_batch, frames, patches, heads, DH)
    q_h = queries.reshape(shape)
    k_h = keys.reshape(shape)
    v_h = values.reshape(shape)
    g_h = grad_attn.reshape(shape)
    scale = DH ** (-0.5)
    f32 = jnp.float32
    scores = jnp.einsum("bfphd,bgphd->bphfg", q_h, k_h, preferred_element_type=f32) * scale
    top = jnp.max(scores, axis=-1, keepdims=True)
    expos = jnp.exp(scores - top)
    probs = expos / jnp.sum(expos, axis=-1, keepdims=True)
    probs_b = probs.astype(jnp.bfloat16)
    attn_out = jnp.einsum("bphfg,bgphd->bfphd", probs_b, v_h, preferred_element_type=f32).astype(
        jnp.bfloat16
    )
    dprobs = jnp.einsum("bfphd,bgphd->bphfg", g_h, v_h, preferred_element_type=f32)
    delta = jnp.sum(probs * dprobs, axis=-1, keepdims=True)
    dscores = (probs * (dprobs - delta) * scale).astype(jnp.bfloat16)
    grad_q = jnp.einsum("bphfg,bgphd->bfphd", dscores, k_h, preferred_element_type=f32).astype(
        jnp.bfloat16
    )
    grad_k = jnp.einsum("bphfg,bfphd->bgphd", dscores, q_h, preferred_element_type=f32).astype(
        jnp.bfloat16
    )
    grad_v = jnp.einsum("bphfg,bfphd->bgphd", probs_b, g_h, preferred_element_type=f32).astype(
        jnp.bfloat16
    )
    flat = (video_batch, frames, patches, width)
    return (
        grad_q.reshape(flat),
        grad_k.reshape(flat),
        grad_v.reshape(flat),
        attn_out.reshape(flat),
    )


def on_device(layer_input, cotangent, queries, keys, values, gain, w_qkv, w_out):
    video_batch, frames_dev, patches, width = layer_input.shape
    total = video_batch * frames_dev * patches
    cols = w_out.shape[0]
    flat_cot = cotangent.reshape(total, width)
    grad_attn = jnp.einsum(
        "rd,cd->rc",
        flat_cot,
        lax.all_gather(w_out, "seq", axis=1, tiled=True),
        preferred_element_type=jnp.float32,
    )
    grad_attn = grad_attn.astype(jnp.bfloat16).reshape(video_batch, frames_dev, patches, cols)
    patch_grad = lax.all_to_all(grad_attn, "seq", split_axis=2, concat_axis=1, tiled=True)
    grad_q, grad_k, grad_v, attn_out = attend_grad(queries, keys, values, patch_grad)
    grad_q, grad_k, grad_v, attn_out = (
        lax.all_to_all(grad_q, "seq", split_axis=1, concat_axis=2, tiled=True),
        lax.all_to_all(grad_k, "seq", split_axis=1, concat_axis=2, tiled=True),
        lax.all_to_all(grad_v, "seq", split_axis=1, concat_axis=2, tiled=True),
        lax.all_to_all(attn_out, "seq", split_axis=1, concat_axis=2, tiled=True),
    )
    proj_grad = jnp.stack([grad_q, grad_k, grad_v], axis=3).reshape(total, 3 * cols)
    attn_rows = attn_out.reshape(total, cols)
    x32 = layer_input.reshape(total, width).astype(jnp.float32)
    input_mean = jnp.mean(x32, axis=1, keepdims=True)
    centered_input = x32 - input_mean
    inverse_deviation = 1.0 / jnp.sqrt(
        jnp.mean(centered_input * centered_input, axis=1, keepdims=True) + 1e-06
    )
    standardized_input = centered_input * inverse_deviation
    normed_input = (standardized_input * gain).astype(jnp.bfloat16)
    piece = lax.all_gather(w_qkv, "seq", axis=0, tiled=True)
    norm_output_gradient = jnp.einsum(
        "rk,dk->rd",
        proj_grad,
        piece.reshape(piece.shape[0], 3 * cols),
        preferred_element_type=jnp.float32,
    )
    owned = w_qkv.shape[0]
    qkv_full = jnp.einsum("rd,rk->dk", normed_input, proj_grad, preferred_element_type=jnp.float32)
    out_full = jnp.einsum("rc,rd->cd", attn_rows, flat_cot, preferred_element_type=jnp.float32)
    grad_wqkv = lax.psum_scatter(qkv_full, "seq", scatter_dimension=0, tiled=True)
    grad_wout = lax.psum_scatter(out_full, "seq", scatter_dimension=1, tiled=True)
    grad_wqkv = grad_wqkv.reshape(owned, 3, cols)
    local_portion = width // lax.axis_size("head")
    start_offset = lax.axis_index("head") * local_portion
    standardized_portion = lax.dynamic_slice_in_dim(
        standardized_input, start_offset, local_portion, 1
    )
    gain_part = lax.dynamic_slice_in_dim(gain, start_offset, local_portion, 0)
    full_grad = lax.psum(norm_output_gradient, "head")
    scaled_gradient_whole = full_grad * gain
    gradient_mean = jnp.mean(scaled_gradient_whole, axis=1, keepdims=True)
    gradient_normed_mean = jnp.mean(
        scaled_gradient_whole * standardized_input, axis=1, keepdims=True
    )
    partial_gradient = lax.dynamic_slice_in_dim(full_grad, start_offset, local_portion, 1)
    scaled_gradient = partial_gradient * gain_part
    branch_input_gradient = (
        inverse_deviation
        * (scaled_gradient - gradient_mean - standardized_portion * gradient_normed_mean)
    ).astype(jnp.bfloat16)
    branch_input_gradient = branch_input_gradient.reshape(
        video_batch, frames_dev, patches, local_portion
    )
    gain_gradient = lax.psum(jnp.sum(partial_gradient * standardized_portion, axis=0), "seq")
    return (branch_input_gradient, grad_wqkv, grad_wout, gain_gradient)


def solution(mesh):
    in_specs = (
        P(None, "seq", None, None),
        P(None, "seq", None, None),
        P(None, None, "seq", "head"),
        P(None, None, "seq", "head"),
        P(None, None, "seq", "head"),
        P(),
        P("seq", None, "head"),
        P("head", "seq"),
    )
    out_specs = (P(None, "seq", None, "head"), P("seq", None, "head"), P("head", "seq"), P("head"))
    return jax.shard_map(
        on_device, mesh=mesh, in_specs=in_specs, out_specs=out_specs, check_vma=False
    )
```

profile of v0, /device:TPU:2, one launch (start us, length us, event | category | flops | bytes accessed | tf_op | source)
XLA Modules:
  0.0 1395.1 jit_solution(8688765751712645860)
XLA Ops:
  8.8 189.3 %all-gather = bf16[64,20,320]{2,1,0:T(8,128)(2,1)S(1)} all-gather(bf16[1,20,320]{2,1,0:T(8,128)(2,1)} %bitcast.119), channel_id=1, replica_groups=mesh['seq'=64,'head'=4] {'seq'}, dimensions={0}, use_global_device_ids=true | all-gather | bytes 832000 | tf_op jit(solution)/shard_map/all_gather | solution.py:56
  202.6 16.9 %all-to-all-start = ((bf16[1,2,256,320]{3,1,0,2:T(2,128)(2,1)}), bf16[1,2,256,320]{3,1,0,2:T(2,128)(2,1)S(1)}, u32[]{:S(2)}, u32[]{:S(2)}) async-start(bf16[1,2,256,320]{3,1,0,2:T(2,128)(2,1)} %copy.39), calls=%async_computation | async-start | bytes 786432 | tf_op jit(solution)/shard_map/all_to_all | solution.py:60
  219.6 2.5 fusion.27
  223.7 8.5 all-to-all-done
  232.2 6.5 all-to-all-start.4
  241.1 3.6 convolution_convert_fusion.1
  246.7 5.6 all-to-all-done.4
  252.3 5.7 all-to-all-start.1
  258.2 3.5 convolution_convert_fusion.3
  263.7 7.3 all-to-all-done.1
  271.0 6.9 all-to-all-start.2
  278.4 2.7 convolution_convert_fusion.2
  285.8 5.2 all-to-all-done.2
  291.0 6.1 all-to-all-start.3
  297.2 3.3 fusion.31
  304.4 5.9 all-to-all-done.3
  310.6 3.8 pad_maximum_fusion
  314.4 4.9 copy.52
  321.7 5.2 fusion.30
  326.9 44.2 %all-gather.3.cloned.1.call-done = bf16[1280,3,320]{2,1,0:T(4,128)(2,1)} async-done(((bf16[20,3,320]{2,1,0:T(4,128)(2,1)}), bf16[1280,3,320]{2,1,0:T(4,128)(2,1)}) %all-gather.3.cloned.1.call-update) | async-done | bytes 2457616 | tf_op jit(solution)/shard_map/all_gather | solution.py:78
  371.1 7.5 copy.54
  378.6 5.1 fusion.29
  383.7 224.4 %fusion = f32[24,960]{1,0:T(8,128)S(1)} fusion(f32[1280,960]{1,0:T(8,128)} %fusion.30), kind=kCustom, calls=%all-reduce-scatter | all-reduce-scatter fusion | flops 1474561 | bytes 5008384
  619.2 3.2 collective-permute-start.5
  622.7 11.6 collective-permute-start.6
  635.7 11.6 collective-permute-start.8
  647.3 11.6 collective-permute-start.9
  660.9 17.9 %concatenate = f32[276,960]{1,0:T(8,128)} concatenate(f32[12,960]{1,0:T(8,128)} %copy-done.5, f32[24,960]{1,0:T(8,128)} %collective-permute-done.9, f32[24,960]{1,0:T(8,128)} %collective-permute-done.8, f32[24,960]{1,0:T(8,128)S(1)} %collective-permute-done.7, f32[24,960]{1,0:T(8,128)S(1)} %collective-permute-done.6, f32[24,960]{1,0:T(8,128)S(1)} %collective-permute-done.5, ...), dimensions={0} | concatenate | bytes 2119680
  680.5 408.2 %all-reduce.8.cloned.1.call-done = f32[320,1280]{0,1:T(8,128)} async-done(((f32[320,1280]{0,1:T(8,128)}), f32[320,1280]{0,1:T(8,128)}) %all-reduce.8.cloned.1.call-update) | async-done | bytes 1638416
  1090.1 114.3 %all-reduce.6.cloned.1.call-done = f32[512,1280]{1,0:T(8,128)} async-done(((f32[512,1280]{1,0:T(8,128)}), f32[512,1280]{1,0:T(8,128)}) %all-reduce.6.cloned.1.call-update) | async-done | bytes 2621456 | tf_op jit(solution)/shard_map/psum | solution.py:97
  1204.4 2.6 multiply_reduce_fusion.2
  1209.9 178.7 %psum.15 = f32[320]{0:T(512)} all-reduce(f32[320]{0:T(512)S(1)} %get-tuple-element.18), channel_id=1, replica_groups=mesh['seq'=64,'head'=4] {'seq'}, use_global_device_ids=true, to_apply=%region_11.0 | all-reduce | flops 320 | bytes 2560 | tf_op jit(solution)/shard_map/psum | solution.py:112
  (81 shorter events, 45.5 us)
Async XLA Ops:
  7.2 192.2 %copy-start = (bf16[1,2,256,1280]{3,2,1,0:T(8,128)(2,1)S(1)}, bf16[1,2,256,1280]{3,2,1,0:T(8,128)(2,1)}, u32[]{:S(2)}) copy-start(bf16[1,2,256,1280]{3,2,1,0:T(8,128)(2,1)} %param.9) | copy-start | bytes 3932164
  7.2 364.0 %all-gather.3.cloned.1.call-start = ((), (), s32[]{:S(2)}) async-start(), calls=%async_computation.5 | async-start | bytes 3993600 | tf_op jit(solution)/shard_map/all_gather | solution.py:78
  199.3 20.2 %copy-start.8 = (bf16[1,128,4,320]{1,3,2,0:T(8,128)(2,1)S(1)}, bf16[1,128,4,320]{1,3,2,0:T(8,128)(2,1)}, u32[]{:S(2)}) copy-start(bf16[1,128,4,320]{1,3,2,0:T(8,128)(2,1)} %param.10) | copy-start | bytes 983044
  201.2 20.8 %copy-start.4 = (bf16[1,128,4,320]{1,3,2,0:T(8,128)(2,1)S(1)}, bf16[1,128,4,320]{1,3,2,0:T(8,128)(2,1)}, u32[]{:S(2)}) copy-start(bf16[1,128,4,320]{1,3,2,0:T(8,128)(2,1)} %param.12) | copy-start | bytes 983044
  201.3 20.7 %copy-start.9 = (bf16[1,128,4,320]{1,3,2,0:T(8,128)(2,1)S(1)}, bf16[1,128,4,320]{1,3,2,0:T(8,128)(2,1)}, u32[]{:S(2)}) copy-start(bf16[1,128,4,320]{1,3,2,0:T(8,128)(2,1)} %param.11) | copy-start | bytes 983044
  202.6 29.6 %all-to-all-start = ((bf16[1,2,256,320]{3,1,0,2:T(2,128)(2,1)}), bf16[1,2,256,320]{3,1,0,2:T(2,128)(2,1)S(1)}, u32[]{:S(2)}, u32[]{:S(2)}) async-start(bf16[1,2,256,320]{3,1,0,2:T(2,128)(2,1)} %copy.39), calls=%async_computation | async-start | bytes 786432 | tf_op jit(solution)/shard_map/all_to_all | solution.py:60
  232.2 20.0 %all-to-all-start.4 = ((bf16[1,128,4,320]{3,2,0,1:T(4,128)(2,1)}), bf16[1,128,4,320]{3,2,0,1:T(4,128)(2,1)S(1)}, u32[]{:S(2)}, u32[]{:S(2)}) async-start(bf16[1,128,4,320]{3,2,0,1:T(4,128)(2,1)} %copy.56), calls=%async_computation.4 | async-start | bytes 786432 | tf_op jit(solution)/shard_map/all_to_all | solution.py:66
  239.7 5.0 copy-start.3
  241.1 16.8 %copy-start.1 = (bf16[1,2,256,1280]{3,2,1,0:T(8,128)(2,1)S(1)}, bf16[1,2,256,1280]{3,2,1,0:T(8,128)(2,1)}, u32[]{:S(2)}) copy-start(bf16[1,2,256,1280]{3,2,1,0:T(8,128)(2,1)} %param.8) | copy-start | bytes 3932164
  252.3 18.7 %all-to-all-start.1 = ((bf16[1,128,4,320]{3,2,0,1:T(4,128)(2,1)}), bf16[1,128,4,320]{3,2,0,1:T(4,128)(2,1)S(1)}, u32[]{:S(2)}, u32[]{:S(2)}) async-start(bf16[1,128,4,320]{3,2,0,1:T(4,128)(2,1)} %copy.43), calls=%async_computation.1 | async-start | bytes 786432 | tf_op jit(solution)/shard_map/all_to_all | solution.py:63
  271.0 20.0 %all-to-all-start.2 = ((bf16[1,128,4,320]{3,2,0,1:T(4,128)(2,1)}), bf16[1,128,4,320]{3,2,0,1:T(4,128)(2,1)}, u32[]{:S(2)}, u32[]{:S(2)}) async-start(bf16[1,128,4,320]{3,2,0,1:T(4,128)(2,1)} %copy.46), calls=%async_computation.2 | async-start | bytes 786432 | tf_op jit(solution)/shard_map/all_to_all | solution.py:64
  291.0 19.3 %all-to-all-start.3 = ((bf16[1,128,4,320]{3,2,0,1:T(4,128)(2,1)}), bf16[1,128,4,320]{3,2,0,1:T(4,128)(2,1)S(1)}, u32[]{:S(2)}, u32[]{:S(2)}) async-start(bf16[1,128,4,320]{3,2,0,1:T(4,128)(2,1)} %copy.50), calls=%async_computation.3 | async-start | bytes 786432 | tf_op jit(solution)/shard_map/all_to_all | solution.py:65
  297.1 3.4 copy-start.6
  297.1 791.5 %all-reduce.8.cloned.1.call-start = ((), (), s32[]{:S(2)}) async-start(), calls=%async_computation.7 | async-start | bytes 3932160
  300.5 903.9 %all-reduce.6.cloned.1.call-start = ((), (), s32[]{:S(2)}) async-start(), calls=%async_computation.6 | async-start | bytes 5242880 | tf_op jit(solution)/shard_map/psum | solution.py:97
  320.8 1.0 copy-start.2
  383.7 275.3 %copy-start.7 = (u32[256]{0:T(256)S(1)}, u32[256]{0:T(256)}, u32[]{:S(2)}) copy-start(u32[256]{0:T(256)} %constant.34) | copy-start | bytes 3076
  608.1 9.0 collective-permute-start.10
  609.4 9.8 collective-permute-start
  611.4 11.4 collective-permute-start.1
  613.3 21.1 %collective-permute-start.2 = (f32[24,960]{1,0:T(8,128)S(1)}, f32[24,960]{1,0:T(8,128)S(1)}, u32[]{:S(2)}, u32[]{:S(2)}) collective-permute-start(f32[24,960]{1,0:T(8,128)S(1)} %fusion), channel_id=1, source_target_pairs={{0,12},{4,16},{8,20},{12,24},{16,28},{20,32},{24,36},{28,40},{32,4... | collective-permute-start | bytes 276488
  615.2 20.5 %collective-permute-start.3 = (f32[24,960]{1,0:T(8,128)S(1)}, f32[24,960]{1,0:T(8,128)S(1)}, u32[]{:S(2)}, u32[]{:S(2)}) collective-permute-start(f32[24,960]{1,0:T(8,128)S(1)} %fusion), channel_id=1, source_target_pairs={{0,16},{4,20},{8,24},{12,28},{16,32},{20,36},{24,40},{28,44},{32,4... | collective-permute-start | bytes 276488
  617.2 30.1 %copy-start.5 = (f32[12,960]{1,0:T(8,128)}, f32[12,960]{1,0:T(8,128)S(1)}, u32[]{:S(2)}) copy-start(f32[12,960]{1,0:T(8,128)S(1)} %collective-permute-done.10) | copy-start | bytes 138244
  617.2 30.1 %collective-permute-start.4 = (f32[24,960]{1,0:T(8,128)S(1)}, f32[24,960]{1,0:T(8,128)S(1)}, u32[]{:S(2)}, u32[]{:S(2)}) collective-permute-start(f32[24,960]{1,0:T(8,128)S(1)} %fusion), channel_id=1, source_target_pairs={{0,20},{4,24},{8,28},{12,32},{16,36},{20,40},{24,44},{28,48},{32,5... | collective-permute-start | bytes 276488
  619.2 41.6 %collective-permute-start.5 = (f32[24,960]{1,0:T(8,128)S(1)}, f32[24,960]{1,0:T(8,128)S(1)}, u32[]{:S(2)}, u32[]{:S(2)}) collective-permute-start(f32[24,960]{1,0:T(8,128)S(1)} %fusion), channel_id=1, source_target_pairs={{0,24},{4,28},{8,32},{12,36},{16,40},{20,44},{24,48},{28,52},{32,5... | collective-permute-start | bytes 276488
  622.7 38.1 %collective-permute-start.6 = (f32[24,960]{1,0:T(8,128)S(1)}, f32[24,960]{1,0:T(8,128)S(1)}, u32[]{:S(2)}, u32[]{:S(2)}) collective-permute-start(f32[24,960]{1,0:T(8,128)S(1)} %fusion), channel_id=1, source_target_pairs={{0,28},{4,32},{8,36},{12,40},{16,44},{20,48},{24,52},{28,56},{32,6... | collective-permute-start | bytes 276488
  634.4 26.5 %collective-permute-start.7 = (f32[24,960]{1,0:T(8,128)S(1)}, f32[24,960]{1,0:T(8,128)S(1)}, u32[]{:S(2)}, u32[]{:S(2)}) collective-permute-start(f32[24,960]{1,0:T(8,128)S(1)} %fusion), channel_id=1, source_target_pairs={{0,32},{4,36},{8,40},{12,44},{16,48},{20,52},{24,56},{28,60},{32,6... | collective-permute-start | bytes 276488
  635.7 25.2 %collective-permute-start.8 = (f32[24,960]{1,0:T(8,128)S(1)}, f32[24,960]{1,0:T(8,128)}, u32[]{:S(2)}, u32[]{:S(2)}) collective-permute-start(f32[24,960]{1,0:T(8,128)S(1)} %fusion), channel_id=1, source_target_pairs={{0,36},{4,40},{8,44},{12,48},{16,52},{20,56},{24,60},{28,64},{32,6... | collective-permute-start | bytes 276488
  647.3 13.6 collective-permute-start.9
Sparse Core Ops, SparseCore 0:
  10.4 360.7 all-gather.2
  373.8 714.8 all-reduce.7
  1091.6 112.8 all-reduce.5
where the time goes:
time: 1410 us; the launch traced here: 1400 us
  waiting for transfers between devices  600 us (43%)
  blocking collectives  592 us (42%)
  starting transfers between devices  91.8 us (7%)
  local copies, waits for them, and re-layouts  54.8 us (4%)
  matrix products  29.8 us (2%)
  between operations  15.4 us (1%)
    unnamed x15, waiting for transfers between devices  409 us
    unnamed x1, blocking collectives  224 us
    all_gather x1, blocking collectives, on_device(): lax.all_gather(w_out, 'seq', axis=1, tiled=True)  189 us
    psum x1, blocking collectives, on_device(): lax.psum(jnp.sum(partial_gradient * standardized_portion, axis=0), 'seq')  179 us
    psum x1, waiting for transfers between devices, on_device(): full_grad = lax.psum(norm_output_gradient, 'head')  114 us
    unnamed x12, starting transfers between devices  49.6 us
    all_gather x1, waiting for transfers between devices, on_device(): piece = lax.all_gather(w_qkv, 'seq', axis=0, tiled=True)  44.2 us
  transfers between devices with their start and end apart: 19, of which 10 were waited for; matrix products, arithmetic and copies ran while one was open for 22% of the time, Pallas kernels for 0%

commit v1 on v0

v1 whole, which is shorter than its diff:
```python
import jax
import jax.numpy as jnp
from jax import lax
from jax.experimental import pallas as pl
from jax.experimental.pallas import tpu as pltpu
from jax.sharding import Mesh
from jax.sharding import PartitionSpec as P

F32, BF16 = jnp.float32, jnp.bfloat16
WIDTH = 1280
HALF = WIDTH // 2
COLS = 320
WIDE = 384
DH = 80
HEADS = COLS // DH
TOKENS = 512
FRAMES, PATCHES = 128, 4
SEQ = ("y", "x", "zl")
PLANE = ("y", "x")
OWNED = 20
EPS = 1e-06
NN, NT, TN = ((1,), (0,)), ((1,), (1,)), ((0,), (0,))


def dot(a, b, dims):
    return lax.dot_general(a, b, (dims, ((), ())), preferred_element_type=F32)


def one_hot(source):
    row = lax.broadcasted_iota(jnp.int32, (TOKENS, TOKENS), 0)
    col = lax.broadcasted_iota(jnp.int32, (TOKENS, TOKENS), 1)
    return jnp.where(col == source(row), 1.0, 0.0).astype(BF16)


def call(kernel, out, scratch=(), vmem=48, flops=0, nbytes=0):
    return pl.pallas_call(
        kernel,
        out_shape=[jax.ShapeDtypeStruct(shape, dtype) for shape, dtype in out],
        scratch_shapes=[pltpu.VMEM(shape, dtype) for shape, dtype in scratch],
        compiler_params=pltpu.CompilerParams(vmem_limit_bytes=vmem * 2**20),
        cost_estimate=pl.CostEstimate(flops=flops, bytes_accessed=nbytes, transcendentals=0),
    )


def halves():
    core = lax.axis_index("core")
    mine = pl.ds(pl.multiple_of(core * HALF, 128), HALF)
    theirs = pl.ds(pl.multiple_of((1 - core) * HALF, 128), HALF)
    return mine, theirs


def pack_kernel(x_ref, cot_ref, out_ref):
    mine, _ = halves()
    order = one_hot(lambda r: ((r >> 2) & 1) * 256 + (r >> 3) * 4 + (r & 3))
    out_ref[:, :HALF] = dot(order, cot_ref[:, mine], NN).astype(BF16)
    out_ref[:, HALF:] = dot(order, x_ref[:, mine], NN).astype(BF16)


def standardized(x):
    x = x.astype(F32)
    centered = x - jnp.mean(x, axis=1, keepdims=True)
    rstd = 1.0 / jnp.sqrt(jnp.mean(centered * centered, axis=1, keepdims=True) + EPS)
    return centered * rstd, rstd


def main_kernel(own_ref, other_ref, q_ref, k_ref, v_ref, wo_ref, gain_ref, m_ref, pg_ref, x_s, c_s, g_s, d_s, n_s):
    mine, theirs = halves()
    c_s[:, mine] = own_ref[:, :HALF]
    c_s[:, theirs] = other_ref[:, :HALF]
    x_s[:, mine] = own_ref[:, HALF:]
    x_s[:, theirs] = other_ref[:, HALF:]
    order = one_hot(lambda r: (r & 3) * FRAMES + (r >> 2))
    g_tok = dot(c_s[...], wo_ref[...], NN).astype(BF16)
    g_s[...] = dot(g_tok, order, TN).astype(BF16)
    scale = DH ** (-0.5)
    for p in range(PATCHES):
        lanes = slice(FRAMES * p, FRAMES * (p + 1))
        for h in range(HEADS):
            rows = slice(DH * h, DH * (h + 1))
            q, k, v = q_ref[p, rows, :], k_ref[p, rows, :], v_ref[p, rows, :]
            g = g_s[rows, lanes]
            scores = dot(k, q, TN) * scale
            expos = jnp.exp(scores - jnp.max(scores, axis=0, keepdims=True))
            probs = expos * (1.0 / jnp.sum(expos, axis=0, keepdims=True))
            probs_b = probs.astype(BF16)
            dprobs = dot(v, g, TN)
            delta = jnp.sum(probs * dprobs, axis=0, keepdims=True)
            dscores = (probs * (dprobs - delta) * scale).astype(BF16)
            d_s[0, rows, lanes] = dot(k, dscores, NN).astype(BF16)
            d_s[1, rows, lanes] = dot(q, dscores, NT).astype(BF16)
            d_s[2, rows, lanes] = dot(g, probs_b, NT).astype(BF16)
            d_s[3, rows, lanes] = dot(v, probs_b, NN).astype(BF16)
    for r in range(0, TOKENS, 128):
        xhat, _ = standardized(x_s[r : r + 128, :])
        n_s[r : r + 128, :] = (xhat * gain_ref[...]).astype(BF16)
    for j in range(4):
        tok = dot(order, d_s[j], NT).astype(BF16)
        if j < 3:
            pg_ref[j] = tok
        m = dot(n_s[...] if j < 3 else c_s[...], tok, TN)
        for b in range(16):
            m_ref[b, j] = m[80 * b : 80 * (b + 1)].astype(BF16)


def norm_kernel(own_ref, other_ref, pg_ref, w_ref, gain_ref, keep_ref, send_ref, xh_ref, x_s, w_s):
    mine, theirs = halves()
    core, zh = lax.axis_index("core"), lax.axis_index("zh")
    x_s[:, mine] = own_ref[:, HALF:]
    x_s[:, theirs] = other_ref[:, HALF:]
    for b in range(16):
        for j in range(3):
            w_s[j, 80 * b : 80 * (b + 1), :] = w_ref[b, j]
    step = 128
    lane = lax.broadcasted_iota(jnp.int32, (step, WIDE - COLS), 1)

    def columns(values):
        out = jnp.zeros((step, WIDE - COLS), F32)
        for i, value in enumerate(values):
            out = jnp.where(lane == i, value, out)
        return out

    for r in range(0, TOKENS, step):
        rows = slice(r, r + step)
        xhat, rstd = standardized(x_s[rows, :])
        grad = dot(pg_ref[0, rows, :], w_s[0], NT)
        grad += dot(pg_ref[1, rows, :], w_s[1], NT)
        grad += dot(pg_ref[2, rows, :], w_s[2], NT)
        scaled = grad * gain_ref[...]
        a = jnp.sum(scaled, axis=1, keepdims=True)
        b = jnp.sum(scaled * xhat, axis=1, keepdims=True)
        a_hi, b_hi = a.astype(BF16).astype(F32), b.astype(BF16).astype(F32)
        sums = columns([a, b])
        split = columns([a_hi, a - a_hi, b_hi, b - b_hi]).astype(BF16)
        for z in range(2):
            keep_ref[z, rows, COLS:] = sums
            send_ref[z, rows, COLS:] = split
            for c in range(2):
                cols = slice(COLS * (2 * z + c), COLS * (2 * z + c + 1))

                @pl.when(core == c)
                def _():
                    keep_ref[z, rows, :COLS] = grad[:, cols]

                @pl.when(core != c)
                def _():
                    send_ref[z, rows, :COLS] = grad[:, cols].astype(BF16)

                @pl.when((core == c) & (zh == z))
                def _():
                    xh_ref[rows, :COLS] = xhat[:, cols]

        xh_ref[rows, COLS:] = columns([rstd])


def total(keep, got):
    got = got.astype(F32)
    a = keep[:, COLS : COLS + 1] + got[:, COLS : COLS + 1] + got[:, COLS + 1 : COLS + 2]
    b = keep[:, COLS + 1 : COLS + 2] + got[:, COLS + 2 : COLS + 3] + got[:, COLS + 3 : COLS + 4]
    return keep[:, :COLS] + got[:, :COLS], a, b


def side(values):
    lane = lax.broadcasted_iota(jnp.int32, (TOKENS, WIDE - COLS), 1)
    out = jnp.zeros((TOKENS, WIDE - COLS), F32)
    for i, value in enumerate(values):
        out = jnp.where(lane == i, value, out)
    return out


def combine_kernel(keep_ref, got_ref, own_ref, send_ref):
    zh = lax.axis_index("zh")
    grad, a, b = total(keep_ref[zh], got_ref[zh])
    own_ref[:, :COLS] = grad
    own_ref[:, COLS:] = side([a, b])
    grad, a, b = total(keep_ref[1 - zh], got_ref[1 - zh])
    a_hi, b_hi = a.astype(BF16).astype(F32), b.astype(BF16).astype(F32)
    send_ref[:, :COLS] = grad.astype(BF16)
    send_ref[:, COLS:] = side([a_hi, a - a_hi, b_hi, b - b_hi]).astype(BF16)


def layer_norm_kernel(own_ref, got_ref, xh_ref, gain_ref, out_ref):
    head = lax.axis_index("zh") * 2 + lax.axis_index("core")
    grad, a, b = total(own_ref[...], got_ref[...])
    xhat = xh_ref[:, :COLS]
    rstd = xh_ref[:, COLS : COLS + 1]
    scaled = grad * gain_ref[pl.ds(head, 1), :]
    result = rstd * (scaled - a * (1.0 / WIDTH) - xhat * (b * (1.0 / WIDTH)))
    out_ref[:, :COLS] = result.astype(BF16)
    gains = jnp.sum(grad * xhat, axis=0, keepdims=True)
    spare = WIDE - COLS
    parts = [gains[:, spare * i : spare * (i + 1)] for i in range(5)]
    block = jnp.concatenate(parts + [jnp.zeros((3, spare), F32)], axis=0)
    out_ref[:, COLS:] = jnp.broadcast_to(block[None], (64, 8, spare)).reshape(TOKENS, spare).astype(BF16)


def plane_sum_kernel(got_ref, out_ref):
    for j in range(4):
        acc = got_ref[0, j].astype(F32)
        for b in range(1, 16):
            acc += got_ref[b, j].astype(F32)
        for z in range(4):
            out_ref[z, j] = acc[OWNED * z : OWNED * (z + 1)].astype(BF16)


def line_sum_kernel(got_ref, qkv_ref, wout_ref):
    for j in range(4):
        acc = got_ref[0, j].astype(F32)
        for z in range(1, 4):
            acc += got_ref[z, j].astype(F32)
        if j < 3:
            qkv_ref[j] = acc
        else:
            wout_ref[...] = acc


def unpack_kernel(got_ref, out_ref, gain_ref):
    order = one_hot(lambda r: ((r >> 2) & 63) * 8 + (r >> 8) * 4 + (r & 3))
    out_ref[...] = dot(order, got_ref[:, :COLS], NN).astype(BF16)
    spare = WIDE - COLS
    gain_ref[...] = jnp.sum(got_ref[:, COLS:].astype(F32).reshape(64, 8, spare), axis=0)


def gathered_weights(w_qkv, w_out):
    shard = jnp.concatenate([w_qkv.transpose(1, 0, 2), w_out.T[None]], axis=0)
    parts = [shard]
    for step in (1, 2, 3):
        parts.append(lax.ppermute(shard, "zl", [(i, (i + step) % 4) for i in range(4)]))
    parts = jnp.stack(parts)
    z = lax.axis_index("zl")
    ordered = [lax.dynamic_index_in_dim(parts, (z - src) % 4, 0, False) for src in range(4)]
    block = jnp.stack(ordered, axis=1).reshape(4, 4 * OWNED, COLS)
    wo = lax.all_gather(block[3], PLANE).reshape(WIDTH, COLS)
    return wo, lax.all_gather(block[:3], PLANE)


def on_device(layer_input, cotangent, queries, keys, values, gain, w_qkv, w_out):
    wo, w = gathered_weights(w_qkv, w_out)
    (packed,) = call(pack_kernel, [((TOKENS, WIDTH), BF16)], flops=10**9, nbytes=4 * 2**20)(
        layer_input.reshape(TOKENS, WIDTH), cotangent.reshape(TOKENS, WIDTH)
    )
    own = lax.all_to_all(packed.reshape(64, 8, WIDTH), SEQ, 0, 0).reshape(TOKENS, WIDTH)
    other = lax.ppermute(own, "core", [(0, 1), (1, 0)])

    def turned(a):
        return a.reshape(FRAMES, PATCHES, COLS).transpose(1, 2, 0)

    gain_row = gain.reshape(1, WIDTH)
    m, pg = call(
        main_kernel,
        [((16, 4, 80, COLS), BF16), ((3, TOKENS, COLS), BF16)],
        [
            ((TOKENS, WIDTH), BF16),
            ((TOKENS, WIDTH), BF16),
            ((COLS, TOKENS), BF16),
            ((4, COLS, TOKENS), BF16),
            ((TOKENS, WIDTH), BF16),
        ],
        flops=5 * 10**9,
        nbytes=12 * 2**20,
    )(own, other, turned(queries), turned(keys), turned(values), wo, gain_row)
    m_got = lax.all_to_all(m, PLANE, 0, 0)
    keep, send, xh = call(
        norm_kernel,
        [((2, TOKENS, WIDE), F32), ((2, TOKENS, WIDE), BF16), ((TOKENS, WIDE), F32)],
        [((TOKENS, WIDTH), BF16), ((3, WIDTH, COLS), BF16)],
        flops=10**9,
        nbytes=10 * 2**20,
    )(own, other, pg, w, gain_row)
    got = lax.ppermute(send, "core", [(0, 1), (1, 0)])
    mine, send = call(combine_kernel, [((TOKENS, WIDE), F32), ((TOKENS, WIDE), BF16)], nbytes=4 * 2**20)(keep, got)
    got = lax.ppermute(send, "zh", [(0, 1), (1, 0)])
    (result,) = call(layer_norm_kernel, [((TOKENS, WIDE), BF16)], nbytes=3 * 2**20)(mine, got, xh, gain.reshape(4, COLS))
    (m_part,) = call(plane_sum_kernel, [((4, 4, OWNED, COLS), BF16)], nbytes=4 * 2**20)(m_got)
    result = lax.all_to_all(result.reshape(64, 8, WIDE), SEQ, 0, 0).reshape(TOKENS, WIDE)
    m_got = lax.all_to_all(m_part, ("zl",), 0, 0)
    branch, gains = call(unpack_kernel, [((TOKENS, COLS), BF16), ((8, WIDE - COLS), F32)], flops=10**8, nbytes=2**20)(result)
    grad_qkv, grad_out = call(line_sum_kernel, [((3, OWNED, COLS), F32), ((OWNED, COLS), F32)], nbytes=2**19)(m_got)
    return (
        branch.reshape(1, 2, 256, COLS),
        grad_qkv.transpose(1, 0, 2),
        grad_out.T,
        gains[:5].reshape(COLS),
    )


def solution(mesh):
    mesh = Mesh(mesh.devices.reshape(4, 4, 4, 2, 2), ("y", "x", "zl", "zh", "core"))
    head = ("zh", "core")
    in_specs = (
        P(None, SEQ, None, None),
        P(None, SEQ, None, None),
        P(None, None, SEQ, head),
        P(None, None, SEQ, head),
        P(None, None, SEQ, head),
        P(),
        P(SEQ, None, head),
        P(head, SEQ),
    )
    out_specs = (P(None, SEQ, None, head), P(SEQ, None, head), P(head, SEQ), P(head))
    return jax.shard_map(on_device, mesh=mesh, in_specs=in_specs, out_specs=out_specs, check_vma=False)
```

time: 1410 us -> 235 us (0.17); the launches traced: 1400 us -> 235 us
  blocking collectives: 592 us -> 25.8 us
  waiting for transfers between devices: 600 us -> 86.3 us
  local copies, waits for them, and re-layouts: 54.8 us -> 12.1 us
  Pallas kernels: 0 us -> 31.6 us
  matrix products: 29.8 us -> 0 us
  starting transfers between devices: 91.8 us -> 63.2 us
    unnamed x15 -> x1, waiting for transfers between devices: 409 us -> 0.02 us
    unnamed x1 -> x0, blocking collectives: 224 us -> none
    psum x1 -> x0, blocking collectives: 179 us -> none  [on_device(): lax.psum(jnp.sum(partial_gradient * standardized_portion, axis=0), 'seq')]
    all_gather x1, blocking collectives: 189 us -> 25.8 us  [gathered_weights(): wo = lax.all_gather(block[3], PLANE).reshape(WIDTH, COLS)]
    psum x1 -> x0, waiting for transfers between devices: 114 us -> none  [on_device(): full_grad = lax.psum(norm_output_gradient, 'head')]
    unnamed x12 -> x0, starting transfers between devices: 49.6 us -> none
    ppermute x0 -> x6, waiting for transfers between devices: none -> 45.6 us  [the longest x3 30.5 us: gathered_weights(): lax.ppermute(shard, 'zl', [(i, (i + step) % 4) for i in range(4)])]
    pallas_call x0 -> x8, Pallas kernels: none -> 31.6 us  [the longest x1 12.2 us: on_device(): call(main_kernel, [((16, 4, 80, COLS), BF16), ((3, TOKENS, COLS), BF16)],...]
  transfers between devices with their start and end apart: 19 -> 11, of which waited for: 10 -> 8; matrix products, arithmetic and copies ran while one was open for 22% -> 2% of each run, Pallas kernels for 0% -> 12%
where the time goes in v1:
time: 235 us
  waiting for transfers between devices  86.3 us (37%)
  starting transfers between devices  63.2 us (27%)
  Pallas kernels  31.6 us (13%)
  blocking collectives  25.8 us (11%)
  between operations  14.2 us (6%)
  local copies, waits for them, and re-layouts  12.1 us (5%)
    ppermute x3, waiting for transfers between devices, gathered_weights(): lax.ppermute(shard, 'zl', [(i, (i + step) % 4) for i in range(4)])  30.5 us
    all_to_all x1, starting transfers between devices, on_device(): lax.all_to_all(result.reshape(64, 8, WIDE), SEQ, 0, 0).reshape(TOKENS, WIDE)  27.8 us
    all_gather x1, blocking collectives, gathered_weights(): wo = lax.all_gather(block[3], PLANE).reshape(WIDTH, COLS)  25.8 us
    all_gather x1, waiting for transfers between devices, gathered_weights(): return (wo, lax.all_gather(block[:3], PLANE))  23 us
    ppermute x1, waiting for transfers between devices, on_device(): got = lax.ppermute(send, 'zh', [(0, 1), (1, 0)])  12.8 us
    pallas_call x1, Pallas kernels, on_device(): call(main_kernel, [((16, 4, 80, COLS), BF16), ((3, TOKENS, COLS), BF16)],...  12.2 us
    all_to_all x1, starting transfers between devices, on_device(): lax.all_to_all(packed.reshape(64, 8, WIDTH), SEQ, 0, 0)  12.2 us
    pallas_call x1, Pallas kernels, on_device(): call(norm_kernel, [((2, TOKENS, WIDE), F32), ((2, TOKENS, WIDE), BF16), (...  11.4 us
  transfers between devices with their start and end apart: 11, of which 8 were waited for; matrix products, arithmetic and copies ran while one was open for 2% of the time, Pallas kernels for 12%

profile of v1, /device:TPU:2, one launch (start us, length us, event | category | flops | bytes accessed | tf_op | source)
XLA Modules:
  0.0 234.7 jit_solution(17887810245834994675)
XLA Ops:
  7.2 1.3 copy-done.1
  8.5 1.3 copy-done.2
  9.8 2.1 shard_map.111
  11.9 12.2 %all-to-all-start = ((bf16[64,8,1280]{2,1,0:T(8,128)(2,1)}), bf16[64,8,1280]{2,1,0:T(8,128)(2,1)S(1)}, u32[]{:S(2)}, u32[]{:S(2)}) async-start(bf16[64,8,1280]{2,1,0:T(8,128)(2,1)} %bitcast.2), calls=%async_computation | async-start | bytes 2621440 | tf_op jit(solution)/shard_map/all_to_all | solution.py:241
  24.2 1.5 collective-permute-start.1
  25.8 2.4 %collective-permute-start.2 = (bf16[4,20,320]{2,1,0:T(8,128)(2,1)S(1)}, bf16[4,20,320]{2,1,0:T(8,128)(2,1)S(1)}, u32[]{:S(2)}, u32[]{:S(2)}) collective-permute-start(bf16[4,20,320]{2,1,0:T(8,128)(2,1)S(1)} %get-tuple-element.43), channel_id=1, source_target_pairs={{0,8},{4,12},{8,0},{12,4},{1,9},{5,13},{9,1},{13,5},{2,10},{6,14},... | collective-permute-start | bytes 153608 | tf_op jit(solution)/shard_map/ppermute | solution.py:227
  28.1 1.5 collective-permute-start.3
  29.6 21.9 %collective-permute-done.1 = bf16[4,20,320]{2,1,0:T(8,128)(2,1)S(1)} collective-permute-done((bf16[4,20,320]{2,1,0:T(8,128)(2,1)S(1)}, bf16[4,20,320]{2,1,0:T(8,128)(2,1)S(1)}, u32[]{:S(2)}, u32[]{:S(2)}) %collective-permute-start.1) | collective-permute-done | bytes 51232 | tf_op jit(solution)/shard_map/ppermute | solution.py:227
  51.4 8.6 %collective-permute-done.2 = bf16[4,20,320]{2,1,0:T(8,128)(2,1)S(1)} collective-permute-done((bf16[4,20,320]{2,1,0:T(8,128)(2,1)S(1)}, bf16[4,20,320]{2,1,0:T(8,128)(2,1)S(1)}, u32[]{:S(2)}, u32[]{:S(2)}) %collective-permute-start.2) | collective-permute-done | bytes 51232 | tf_op jit(solution)/shard_map/ppermute | solution.py:227
  62.4 1.4 pad_maximum_fusion.4
  63.8 0.9 slice.14
  64.7 25.8 %all_gather.9 = bf16[16,80,320]{2,1,0:T(8,128)(2,1)S(1)} all-gather(bf16[1,80,320]{2,1,0:T(8,128)(2,1)S(1)} %slice.14), channel_id=1, replica_groups=mesh['y'=4,'x'=4,'zl'=4,'zh'=2,'core'=2] {'y','x'}, dimensions={0}, use_global_device_ids=true | all-gather | bytes 870400 | tf_op jit(solution)/shard_map/all_gather | solution.py:232
  90.5 1.0 copy-done.7
  91.5 12.2 %shard_map.112 = (bf16[16,4,80,320]{3,2,1,0:T(8,128)(2,1)}, bf16[3,512,320]{2,1,0:T(8,128)(2,1)S(1)}) custom-call(bf16[512,1280]{1,0:T(8,128)(2,1)S(1)} %bitcast.38, bf16[512,1280]{1,0:T(8,128)(2,1)S(1)} %collective-permute-done.other_ref, bf16[4,320,128]{2,1,0:T(8,128)(2,1)S(1)} %bitcast.46, bf16[4,320,128]{2,1,0:T(8,128)(2,1)S(1)} %bitcast.47, ...), custom_call_target="tpu_custom_call" | custom-call | flops 5000000000 | bytes 12582912 | tf_op jit(solution)/shard_map/pallas_call | solution.py:248
  103.7 1.0 copy-done.3
  104.7 5.7 %all-to-all-start.2 = ((bf16[16,4,80,320]{3,2,1,0:T(8,128)(2,1)}), bf16[16,4,80,320]{3,2,1,0:T(8,128)(2,1)}, u32[]{:S(2)}, u32[]{:S(2)}) async-start(bf16[16,4,80,320]{3,2,1,0:T(8,128)(2,1)} %get-tuple-element.22), calls=%async_computation.2 | async-start | bytes 7864320 | tf_op jit(solution)/shard_map/all_to_all | solution.py:261
  110.5 23.0 %all-gather.2.cloned.1.call-done.w_ref = bf16[16,3,80,320]{3,2,1,0:T(8,128)(2,1)} async-done(((bf16[1,3,80,320]{3,2,1,0:T(8,128)(2,1)}), bf16[16,3,80,320]{3,2,1,0:T(8,128)(2,1)}) %all-gather.2.cloned.1.call-update) | async-done | bytes 2457616 | tf_op jit(solution)/shard_map/all_gather | solution.py:233
  133.4 1.3 copy-done.4
  134.7 11.4 %shard_map.113 = (f32[2,512,384]{2,1,0:T(8,128)}, bf16[2,512,384]{2,1,0:T(8,128)(2,1)S(1)}, f32[512,384]{1,0:T(8,128)S(1)}) custom-call(bf16[512,1280]{1,0:T(8,128)(2,1)S(1)} %bitcast.39, bf16[512,1280]{1,0:T(8,128)(2,1)S(1)} %collective-permute-done.other_ref, bf16[3,512,320]{2,1,0:T(8,128)(2,1)S(1)} %copy-done.4, ...), custom_call_target="tpu_custom_call" | custom-call | flops 1000000000 | bytes 10485760 | tf_op jit(solution)/shard_map/pallas_call | solution.py:262
  146.1 2.3 collective-permute-done.4.got_ref
  148.4 1.4 copy-done
  149.8 0.8 shard_map.114
  150.6 8.6 %collective-permute-start.5 = (bf16[512,384]{1,0:T(8,128)(2,1)S(1)}, bf16[512,384]{1,0:T(8,128)(2,1)S(1)}, u32[]{:S(2)}, u32[]{:S(2)}) collective-permute-start(bf16[512,384]{1,0:T(8,128)(2,1)S(1)} %get-tuple-element.19), channel_id=1, source_target_pairs={{0,2},{2,0},{1,3},{3,1},{4,6},{6,4},{5,7},{7,5},{8,10},{10,8},{9,1... | collective-permute-start | bytes 1179656 | tf_op jit(solution)/shard_map/ppermute | solution.py:271
  159.2 12.8 %collective-permute-done.5.got_ref = bf16[512,384]{1,0:T(8,128)(2,1)S(1)} collective-permute-done((bf16[512,384]{1,0:T(8,128)(2,1)S(1)}, bf16[512,384]{1,0:T(8,128)(2,1)S(1)}, u32[]{:S(2)}, u32[]{:S(2)}) %collective-permute-start.5) | collective-permute-done | bytes 393248 | tf_op jit(solution)/shard_map/ppermute | solution.py:271
  172.0 1.3 shard_map.115
  173.4 27.8 %all-to-all-start.1 = ((bf16[64,8,384]{2,1,0:T(8,128)(2,1)}), bf16[64,8,384]{2,1,0:T(8,128)(2,1)S(1)}, u32[]{:S(2)}, u32[]{:S(2)}) async-start(bf16[64,8,384]{2,1,0:T(8,128)(2,1)} %bitcast.22), calls=%async_computation.1 | async-start | bytes 786432 | tf_op jit(solution)/shard_map/all_to_all | solution.py:274
  201.2 2.6 %shard_map.117 = bf16[4,4,20,320]{3,2,1,0:T(8,128)(2,1)S(1)} custom-call(bf16[16,4,80,320]{3,2,1,0:T(8,128)(2,1)} %all-to-all-done.2.got_ref), custom_call_target="tpu_custom_call" | custom-call | bytes 4194304 | tf_op jit(solution)/shard_map/pallas_call | solution.py:273
  203.9 0.8 copy.14
  204.7 11.1 %all-to-all-done.1 = bf16[64,8,384]{2,1,0:T(8,128)(2,1)S(1)} async-done(((bf16[64,8,384]{2,1,0:T(8,128)(2,1)}), bf16[64,8,384]{2,1,0:T(8,128)(2,1)S(1)}, u32[]{:S(2)}, u32[]{:S(2)}) %all-to-all-start.1) | async-done | bytes 393248 | tf_op jit(solution)/shard_map/all_to_all | solution.py:274
  215.8 3.4 %all-to-all-start.3 = ((bf16[4,4,20,320]{3,1,2,0:T(4,128)(2,1)}), bf16[4,4,20,320]{3,1,2,0:T(4,128)(2,1)S(1)}, u32[]{:S(2)}, u32[]{:S(2)}) async-start(bf16[4,4,20,320]{3,1,2,0:T(4,128)(2,1)} %copy.14), calls=%async_computation.3 | async-start | bytes 491520 | tf_op jit(solution)/shard_map/all_to_all | solution.py:275
  219.6 0.9 copy.16
  221.2 5.9 %all-to-all-done.3 = bf16[4,4,20,320]{3,1,2,0:T(4,128)(2,1)S(1)} async-done(((bf16[4,4,20,320]{3,1,2,0:T(4,128)(2,1)}), bf16[4,4,20,320]{3,1,2,0:T(4,128)(2,1)S(1)}, u32[]{:S(2)}, u32[]{:S(2)}) %all-to-all-start.3) | async-done | bytes 204832 | tf_op jit(solution)/shard_map/all_to_all | solution.py:275
  (37 shorter events, 4.4 us)
Async XLA Ops:
  7.2 1.3 copy-start.1
  8.5 1.3 copy-start.2
  11.9 12.3 %copy-start.9 = (bf16[20,3,320]{2,0,1:T(8,128)(2,1)S(1)}, bf16[20,3,320]{2,0,1:T(8,128)(2,1)}, u32[]{:S(2)}) copy-start(bf16[20,3,320]{2,0,1:T(8,128)(2,1)} %param.14) | copy-start | bytes 115204
  11.9 12.3 %copy-start.11 = (bf16[320,20]{0,1:T(8,128)(2,1)S(1)}, bf16[320,20]{0,1:T(8,128)(2,1)}, u32[]{:S(2)}) copy-start(bf16[320,20]{0,1:T(8,128)(2,1)} %param.15) | copy-start | bytes 38404
  11.9 50.6 %all-to-all-start = ((bf16[64,8,1280]{2,1,0:T(8,128)(2,1)}), bf16[64,8,1280]{2,1,0:T(8,128)(2,1)S(1)}, u32[]{:S(2)}, u32[]{:S(2)}) async-start(bf16[64,8,1280]{2,1,0:T(8,128)(2,1)} %bitcast.2), calls=%async_computation | async-start | bytes 2621440 | tf_op jit(solution)/shard_map/all_to_all | solution.py:241
  24.1 109.3 %all-gather.2.cloned.1.call-start = ((), (), s32[]{:S(2)}) async-start(), calls=%async_computation.4 | async-start | bytes 3133440 | tf_op jit(solution)/shard_map/all_gather | solution.py:233
  24.2 38.3 %copy-start.10 = (f32[1280]{0:T(1024)S(1)}, f32[1280]{0:T(1024)}, u32[]{:S(2)}) copy-start(f32[1280]{0:T(1024)} %param.13) | copy-start | bytes 15364
  24.2 27.2 %collective-permute-start.1 = (bf16[4,20,320]{2,1,0:T(8,128)(2,1)S(1)}, bf16[4,20,320]{2,1,0:T(8,128)(2,1)S(1)}, u32[]{:S(2)}, u32[]{:S(2)}) collective-permute-start(bf16[4,20,320]{2,1,0:T(8,128)(2,1)S(1)} %get-tuple-element.43), channel_id=1, source_target_pairs={{0,4},{4,8},{8,12},{12,0},{1,5},{5,9},{9,13},{13,1},{2,6},{6,10},{... | collective-permute-start | bytes 153608 | tf_op jit(solution)/shard_map/ppermute | solution.py:227
  25.8 34.3 %collective-permute-start.2 = (bf16[4,20,320]{2,1,0:T(8,128)(2,1)S(1)}, bf16[4,20,320]{2,1,0:T(8,128)(2,1)S(1)}, u32[]{:S(2)}, u32[]{:S(2)}) collective-permute-start(bf16[4,20,320]{2,1,0:T(8,128)(2,1)S(1)} %get-tuple-element.43), channel_id=1, source_target_pairs={{0,8},{4,12},{8,0},{12,4},{1,9},{5,13},{9,1},{13,5},{2,10},{6,14},... | collective-permute-start | bytes 153608 | tf_op jit(solution)/shard_map/ppermute | solution.py:227
  28.1 31.9 %collective-permute-start.3 = (bf16[4,20,320]{2,1,0:T(8,128)(2,1)S(1)}, bf16[4,20,320]{2,1,0:T(8,128)(2,1)S(1)}, u32[]{:S(2)}, u32[]{:S(2)}) collective-permute-start(bf16[4,20,320]{2,1,0:T(8,128)(2,1)S(1)} %get-tuple-element.43), channel_id=1, source_target_pairs={{0,12},{4,0},{8,4},{12,8},{1,13},{5,1},{9,5},{13,9},{2,14},{6,2},{... | collective-permute-start | bytes 153608 | tf_op jit(solution)/shard_map/ppermute | solution.py:227
  60.2 0.6 copy-start.8
  60.8 29.7 %copy-start.5 = (bf16[1,128,4,320]{1,3,2,0:T(8,128)(2,1)S(1)}, bf16[1,128,4,320]{1,3,2,0:T(8,128)(2,1)}, u32[]{:S(2)}) copy-start(bf16[1,128,4,320]{1,3,2,0:T(8,128)(2,1)} %param.10) | copy-start | bytes 983044
  60.8 29.7 %copy-start.6 = (bf16[1,128,4,320]{1,3,2,0:T(8,128)(2,1)S(1)}, bf16[1,128,4,320]{1,3,2,0:T(8,128)(2,1)}, u32[]{:S(2)}) copy-start(bf16[1,128,4,320]{1,3,2,0:T(8,128)(2,1)} %param.11) | copy-start | bytes 983044
  62.4 28.1 %collective-permute-start = (bf16[512,1280]{1,0:T(8,128)(2,1)S(1)}, bf16[512,1280]{1,0:T(8,128)(2,1)S(1)}, u32[]{:S(2)}, u32[]{:S(2)}) collective-permute-start(bf16[512,1280]{1,0:T(8,128)(2,1)S(1)} %bitcast.37), channel_id=1, source_target_pairs={{0,1},{1,0},{2,3},{3,2},{4,5},{5,4},{6,7},{7,6},{8,9},{9,8},{10,11... | collective-permute-start | bytes 3932168 | tf_op jit(solution)/shard_map/ppermute | solution.py:242
  90.5 1.0 copy-start.7
  103.7 1.0 copy-start.3
  104.7 68.6 %all-to-all-start.2 = ((bf16[16,4,80,320]{3,2,1,0:T(8,128)(2,1)}), bf16[16,4,80,320]{3,2,1,0:T(8,128)(2,1)}, u32[]{:S(2)}, u32[]{:S(2)}) async-start(bf16[16,4,80,320]{3,2,1,0:T(8,128)(2,1)} %get-tuple-element.22), calls=%async_computation.2 | async-start | bytes 7864320 | tf_op jit(solution)/shard_map/all_to_all | solution.py:261
  133.4 1.3 copy-start.4
  146.1 2.3 collective-permute-start.4
  148.4 1.4 copy-start
  150.6 21.4 %collective-permute-start.5 = (bf16[512,384]{1,0:T(8,128)(2,1)S(1)}, bf16[512,384]{1,0:T(8,128)(2,1)S(1)}, u32[]{:S(2)}, u32[]{:S(2)}) collective-permute-start(bf16[512,384]{1,0:T(8,128)(2,1)S(1)} %get-tuple-element.19), channel_id=1, source_target_pairs={{0,2},{2,0},{1,3},{3,1},{4,6},{6,4},{5,7},{7,5},{8,10},{10,8},{9,1... | collective-permute-start | bytes 1179656 | tf_op jit(solution)/shard_map/ppermute | solution.py:271
  173.4 42.4 %all-to-all-start.1 = ((bf16[64,8,384]{2,1,0:T(8,128)(2,1)}), bf16[64,8,384]{2,1,0:T(8,128)(2,1)S(1)}, u32[]{:S(2)}, u32[]{:S(2)}) async-start(bf16[64,8,384]{2,1,0:T(8,128)(2,1)} %bitcast.22), calls=%async_computation.1 | async-start | bytes 786432 | tf_op jit(solution)/shard_map/all_to_all | solution.py:274
  215.8 11.3 %all-to-all-start.3 = ((bf16[4,4,20,320]{3,1,2,0:T(4,128)(2,1)}), bf16[4,4,20,320]{3,1,2,0:T(4,128)(2,1)S(1)}, u32[]{:S(2)}, u32[]{:S(2)}) async-start(bf16[4,4,20,320]{3,1,2,0:T(4,128)(2,1)} %copy.14), calls=%async_computation.3 | async-start | bytes 491520 | tf_op jit(solution)/shard_map/all_to_all | solution.py:275
Sparse Core Ops, SparseCore 0:
  61.8 71.5 all-gather.1
